TPU v7x, 256 devices: a whole 4x4x8 slice. The times are simulated.
256 devices in a mesh: dp: 16 (over z_hi, y, core), tensor: 16 (over z_lo, x).
Axes of the slice: x: 4, y: 4, z: 8 (z_hi: 2, z_lo: 4; z = z_hi * 4 + z_lo), core: 2. Of those that a mesh axis runs over, the one named last changes fastest.
Arguments:
- layer_input: bfloat16 [12288, 8192], P('dp', 'tensor'), may hold values from -6 to 6
- gate_saved: bfloat16 [12288, 14336], P('dp', 'tensor'), may hold values from -6 to 6
- up_saved: bfloat16 [12288, 14336], P('dp', 'tensor'), may hold values from -6 to 6
- grad_out: bfloat16 [12288, 8192], P('dp', 'tensor'), may hold values from -6 to 6
- down_weight: bfloat16 [14336, 8192], P('tensor', 'dp'), may hold values from -0.046875 to 0.046875
- hidden_proj: bfloat16 [14336, 64], P('tensor'), may hold values from -0.046875 to 0.046875
- model_proj: bfloat16 [8192, 64], P('tensor'), may hold values from -0.0625 to 0.0625
- query_sketch: bfloat16 [4096, 8192], P('dp', 'tensor'), may hold values from -6 to 6
- resp_lengths: int32 [96, 2], P('dp'), may hold values from 16 to 64
- chosen_index: int32 [96], P('dp'), may hold values from 0 to 1
Outputs:
- sketch: float32 [96, 8192], P('dp', 'tensor')
- scores: float32 [96, 4096], P('tensor', 'dp')
All inputs are finite; a program needn't handle non-finite values.
Results may differ from a plain program's by a relative error of at most 0.0095.
Values may be sent and summed in bfloat16 or wider, within the bound.
No kernel may reach another device: no remote copies, remote signals or barrier semaphores. Data moves between devices by JAX's collectives and lax.ppermute only.
A program may use at most 128 MiB of HBM per device.

v0:
```python
import jax
import jax.numpy as jnp
from jax import lax
from jax.experimental import pallas as pl
from jax.experimental.pallas import tpu as pltpu
from jax.sharding import PartitionSpec as P

SCALE = 0.25
AXES = ("dp", "tensor")
F32 = jnp.float32
BF16 = jnp.bfloat16
TRANSPOSED = (((1,), (1,)), ((), ()))


def flat(x, y, z, c):
    return (((z // 4) * 4 + y) * 2 + c) * 16 + (z % 4) * 4 + x


def move(value, where):
    pairs = []
    for z in range(8):
        for y in range(4):
            for x in range(4):
                for c in range(2):
                    nx, ny, nz, nc = where(x, y, z, c)
                    pairs.append((flat(x, y, z, c), flat(nx % 4, ny % 4, nz % 8, nc % 2)))
    return lax.ppermute(value, AXES, pairs)


def side(c):
    return 1 - 2 * c


def ring_x(sign):
    return lambda x, y, z, c: (x + sign * side(c), y, z, c)


def ring_y(sign):
    return lambda x, y, z, c: (x, y + sign * side(c), z, c)


def shift_x(step):
    return lambda x, y, z, c: (x + step, y, z, c)


def shift_y(step):
    return lambda x, y, z, c: (x, y + step, z, c)


def line_z(step):
    return lambda x, y, z, c: (x, y, (z // 4) * 4 + (z + step) % 4, c)


def line_z_both(x, y, z, c):
    return line_z(side(c))(x, y, z, c)


def swap_core(x, y, z, c):
    return (x, y, z, c + 1)


def swap_half(x, y, z, c):
    return (x, y, z + 4, c)


def pick(buffer, index, axis):
    return lax.dynamic_index_in_dim(buffer, index, axis, keepdims=False)


def put(buffer, value, index):
    return lax.dynamic_update_index_in_dim(buffer, value, index, 0)


SLOTS = 4


def product_kernel(count, last, index_ref, *refs):
    pieces, refs = refs[:count], refs[count:]
    near_own, near_other, far_own, far_other, refs = refs[0], refs[1], refs[2:4], refs[4:6], refs[6:]
    early = []
    if last:
        start_hbm, slope_hbm, proj_ref, left_ref, down_ref = refs[:5]
        out_refs, refs = refs[5:9], refs[9:]
        left_buf, right_buf, left_sem, right_sem, sum_ref, start_ref, slope_ref, tail_sem = refs
        early = [
            pltpu.make_async_copy(start_hbm, start_ref, tail_sem.at[0]),
            pltpu.make_async_copy(slope_hbm, slope_ref, tail_sem.at[1]),
        ]
    else:
        sum_ref, left_buf, right_buf, left_sem, right_sem = refs
    half = sum_ref.shape[1] // 2

    def copies(n):
        slot = n % SLOTS
        one = pltpu.make_async_copy(pieces[n], left_buf.at[slot], left_sem.at[slot])
        one.start()
        waits = [one]
        place = index_ref[n]
        for part in range(2):
            rows = pl.ds(part * half, half)
            target = right_buf.at[slot, rows]
            sem = right_sem.at[slot, part]
            for which, source in enumerate(
                (
                    near_own.at[place % 4, rows],
                    near_other.at[place % 4, rows],
                    far_own[part].at[place % 4],
                    far_other[part].at[place % 4],
                )
            ):

                @pl.when(place // 4 == which)
                def _(source=source):
                    pltpu.make_async_copy(source, target, sem).start()

            waits.append(pltpu.make_async_copy(near_own.at[0, rows], target, sem))
        return waits

    ahead = SLOTS - 1
    waits = [copies(n) for n in range(min(ahead, count))]
    for n in range(count):
        if n + ahead < count:
            waits.append(copies(n + ahead))
        elif n + ahead == count:
            for copy in early:
                copy.start()
        for wait in waits[n]:
            wait.wait()
        product = lax.dot_general(
            left_buf[n % SLOTS], right_buf[n % SLOTS], TRANSPOSED, preferred_element_type=F32
        )
        if n:
            sum_ref[...] += product
        else:
            sum_ref[...] = product

    if last:
        column = index_ref[count]
        for copy in early:
            copy.wait()
        pairs = down_ref.shape[0]
        span = left_ref.shape[0] // pairs
        for p in range(pairs):
            here = pl.ds(p * span, span)
            if p % 2 == 0:
                two = pl.ds(p * span, 2 * span)
                total = (sum_ref[two, :] + start_ref[two, :]) * slope_ref[two, :].astype(F32)
                e = jnp.dot(total.astype(BF16), proj_ref[...], preferred_element_type=F32)
                e = e.astype(BF16)
            gates = lax.dot_general(
                left_ref[here, :],
                e[(p % 2) * span : (p % 2 + 1) * span],
                (((0,), (0,)), ((), ())),
                preferred_element_type=F32,
            )
            total = (down_ref[p] + gates).reshape(2, 4, 8, 128)
            for m in range(4):
                for away in range(4):

                    @pl.when((column + away) % 4 == m)
                    def _(m=m, away=away, total=total):
                        out_refs[away][:, p] = total[:, m]


ANYWHERE = pl.BlockSpec(memory_space=pl.ANY)
IN_VMEM = pl.BlockSpec(memory_space=pltpu.VMEM)
IN_SMEM = pl.BlockSpec(memory_space=pltpu.SMEM)


def products(pieces, weights, index, tail=()):
    count = len(pieces)
    rows, depth = pieces[0].shape
    units = weights[0].shape[1]
    last = bool(tail)
    scratch = [
        pltpu.VMEM((SLOTS, rows, depth), BF16),
        pltpu.VMEM((SLOTS, units, depth), BF16),
        pltpu.SemaphoreType.DMA((SLOTS,)),
        pltpu.SemaphoreType.DMA((SLOTS, 2)),
    ]
    out_shape = jax.ShapeDtypeStruct((rows, units), F32)
    out_specs = IN_VMEM
    if last:
        scratch += [
            pltpu.VMEM((rows, units), F32),
            pltpu.VMEM((rows, units), F32),
            pltpu.VMEM((rows, units), BF16),
            pltpu.SemaphoreType.DMA((2,)),
        ]
        out_shape = [jax.ShapeDtypeStruct((2, tail[4].shape[0], 8, 128), F32)] * 4
        out_specs = [IN_VMEM] * 4
    return pl.pallas_call(
        lambda *refs: product_kernel(count, last, *refs),
        out_shape=out_shape,
        in_specs=[IN_SMEM]
        + [ANYWHERE] * (count + len(weights) + min(len(tail), 2))
        + [IN_VMEM] * max(len(tail) - 2, 0),
        out_specs=out_specs,
        scratch_shapes=scratch,
        compiler_params=pltpu.CompilerParams(vmem_limit_bytes=58 * 2**20),
        cost_estimate=pl.CostEstimate(
            flops=2 * count * rows * units * depth,
            bytes_accessed=2 * count * (rows + units) * depth + 4 * rows * units,
            transcendentals=0,
        ),
    )(index, *pieces, *weights, *tail)


def sum_columns(slabs):
    total = slabs[0]
    for step in (1, 2, 3):
        total = total + move(slabs[step], shift_x(step))
    return total


def gather_pairs(value, zh, y, c):
    halves = jnp.zeros((2,) + value.shape, value.dtype)
    halves = put(halves, value, zh)
    halves = put(halves, move(value, swap_half), 1 - zh)
    rows = jnp.zeros((4,) + halves.shape, value.dtype)
    rows = put(rows, halves, y)
    for step in (1, 2, 3):
        rows = put(rows, move(halves, shift_y(step)), (y - step) % 4)
    every = jnp.zeros((2,) + rows.shape, value.dtype)
    every = put(every, rows, c)
    every = put(every, move(rows, swap_core), 1 - c)
    return every


def local(
    layer_input,
    gate_saved,
    up_saved,
    grad_out,
    down_weight,
    hidden_proj,
    model_proj,
    query_sketch,
    resp_lengths,
    chosen_index,
):
    tok_rows = grad_out.shape[0]
    pairs = resp_lengths.shape[0]
    span = tok_rows // pairs
    half = span // 2
    sk = hidden_proj.shape[1]
    entries = 2 * sk * sk
    i = lax.axis_index("dp")
    j = lax.axis_index("tensor")
    zh, y, c = i // 8, (i // 2) % 4, i % 2
    zl, x = j // 4, j % 4
    sign = 1 - 2 * c

    def turn(*values):
        return lax.optimization_barrier(values)

    def along_y(value):
        groups = [[(h * 4 + r) * 2 + k for r in range(4)] for h in range(2) for k in range(2)]
        return lax.all_gather(value, "dp", axis=0, tiled=False, axis_index_groups=groups)

    sixteenth = tok_rows // 16
    mid = down_weight.shape[0] // 2
    near_own = along_y(down_weight)

    terms = jnp.concatenate(
        [
            jnp.dot(grad_out, model_proj, preferred_element_type=F32),
            jnp.dot(layer_input, model_proj, preferred_element_type=F32),
        ],
        axis=1,
    ).astype(BF16)
    dealt = lax.all_to_all(terms, "tensor", 0, 0, tiled=True)
    ahead0 = move(grad_out, ring_x(1))
    behind0 = move(grad_out, ring_x(-1))
    across0 = move(grad_out, shift_x(2))
    hop1 = move(grad_out, line_z_both)
    far_a = move(down_weight[:mid], swap_half)
    ahead0, behind0, across0, hop1, far_a, weight_rows, dealt, near_own = turn(
        ahead0, behind0, across0, hop1, far_a, down_weight, dealt, near_own
    )

    far_own_a = along_y(far_a)
    mine = dealt.reshape(16, sixteenth, 2 * sk).astype(F32).sum(axis=0).astype(BF16)
    ahead1 = move(hop1, ring_x(1))
    behind1 = move(hop1, ring_x(-1))
    across1 = move(hop1, shift_x(2))
    hop2 = move(hop1, line_z_both)
    far_b = move(weight_rows[mid:], swap_half)
    ahead1, behind1, across1, hop2, far_b, far_own_a, mine, gate_saved = turn(
        ahead1, behind1, across1, hop2, far_b, far_own_a, mine, gate_saved
    )

    far_own_b = along_y(far_b)
    full = lax.all_to_all(
        jnp.broadcast_to(mine, (16, sixteenth, 2 * sk)).reshape(tok_rows, 2 * sk),
        "tensor", 0, 0, tiled=True,
    )
    gate32 = gate_saved.astype(F32)
    up32 = up_saved.astype(F32)
    sig = jax.nn.sigmoid(gate32)
    hidden = (gate32 * sig * up32).astype(BF16)
    slope = (up32 * sig * (1.0 + gate32 * (1.0 - sig))).astype(BF16)
    a = jnp.dot(hidden, hidden_proj, preferred_element_type=F32)
    ahead2 = move(hop2, ring_x(1))
    behind2 = move(hop2, ring_x(-1))
    across2 = move(hop2, shift_x(2))
    hop3 = move(hop2, line_z_both)
    near_other = move(near_own, swap_core)
    ahead2, behind2, across2, hop3, near_other, full, slope, a, far_own_b = turn(
        ahead2, behind2, across2, hop3, near_other, full, slope, a, far_own_b
    )
    full = full.astype(F32)

    ahead3 = move(hop3, ring_x(1))
    behind3 = move(hop3, ring_x(-1))
    across3 = move(across2, line_z_both)
    far_other_b = move(far_own_b, swap_core)
    far_other_a = move(far_own_a, swap_core)
    pieces = [
        grad_out, ahead0, behind0, across0,
        hop1, ahead1, behind1, across1,
        hop2, ahead2, behind2, across2,
        hop3, ahead3, behind3, across3,
    ]
    k = jnp.stack(
        [
            ((zl - hop * sign) % 4) * 4 + (x + away) % 4
            for hop in range(4)
            for away in (0, -sign, sign, 2)
        ]
    ).astype(jnp.int32)
    index = jnp.where(k // 8 == zh, 0, 8) + jnp.where(k % 2 == c, 0, 4) + (k // 2) % 4

    slots = jnp.arange(half, dtype=jnp.int32)
    sides = jnp.arange(2, dtype=jnp.int32)
    live = slots[None, None, :] < resp_lengths[:, :, None]
    signs = jnp.where(sides[None, :] == chosen_index[:, None], SCALE, -SCALE).astype(F32)
    weight = jnp.where(live, signs[:, :, None], 0.0).reshape(tok_rows, 1)

    down = jnp.einsum(
        "ptk,ptl->pkl",
        (a * weight).reshape(pairs, span, sk),
        full[:, :sk].reshape(pairs, span, sk),
        precision=lax.Precision.HIGH,
    )
    down = jnp.pad(down, ((0, 0), (0, 0), (0, sk)))
    left = (full[:, sk:] * weight).astype(BF16)
    proj = jnp.pad(hidden_proj, ((0, 0), (sk, 0)))

    weights = (near_own, near_other, far_own_a, far_own_b, far_other_a, far_other_b)
    first = products(pieces[:12], weights, index[:12])
    slabs = products(
        pieces[12:],
        weights,
        jnp.concatenate([index[12:], x.astype(jnp.int32)[None]]),
        (first, slope, proj, left, down),
    )

    both = sum_columns(slabs)
    line = zl % 2
    out = pick(both, line, 0)
    for step in (1, 2, 3):
        out = out + move(pick(both, (line + step) % 2, 0), line_z(step))
    mine = jnp.where(zl >= 2, out[:, :, sk:], out[:, :, :sk])
    sketch = mine.reshape(pairs, 8 * sk)
    every = gather_pairs(sketch, zh, y, c)
    partial = lax.dot_general(
        every.reshape(16 * pairs, 8 * sk),
        query_sketch.astype(F32),
        TRANSPOSED,
        precision=lax.Precision.HIGHEST,
        preferred_element_type=F32,
    ) / jnp.sqrt(F32(entries))
    partial = partial.reshape(2, 2, 2, 2, pairs, -1).transpose(2, 0, 3, 1, 4, 5)
    grid = partial.reshape(4, 4, pairs, -1)
    summed = sum_columns([pick(grid, (x + step) % 4, 0) for step in range(4)])
    scores = pick(summed, zl, 0)
    for step in (1, 2, 3):
        scores = scores + move(pick(summed, (zl + step) % 4, 0), line_z(step))
    return (sketch, scores)


def solution(mesh):
    return jax.shard_map(
        local,
        mesh=mesh,
        in_specs=(
            P("dp", "tensor"),
            P("dp", "tensor"),
            P("dp", "tensor"),
            P("dp", "tensor"),
            P("tensor", "dp"),
            P("tensor", None),
            P("tensor", None),
            P("dp", "tensor"),
            P("dp", None),
            P("dp"),
        ),
        out_specs=(P("dp", "tensor"), P("tensor", "dp")),
        check_vma=False,
    )
```

profile of v0, /device:TPU:24, one launch (start us, length us, event | category | flops | bytes accessed | tf_op | source)
XLA Modules:
  0.0 246.6 jit_solution(315423108943220097)
XLA Ops:
  7.2 0.7 all-gather.7.cloned.1.call-update
  8.0 1.6 collective-permute-start
  9.5 1.7 collective-permute-start.1
  11.3 1.8 collective-permute-start.2
  13.1 1.9 collective-permute-start.3
  15.0 1.0 slice.28
  16.1 6.4 %collective-permute-start.4 = (bf16[448,512]{1,0:T(8,128)(2,1)S(1)}, bf16[448,512]{1,0:T(8,128)(2,1)S(1)}, u32[]{:S(2)}, u32[]{:S(2)}) collective-permute-start(bf16[448,512]{1,0:T(8,128)(2,1)S(1)} %slice.28), channel_id=1, source_target_pairs={{0,128},{16,144},{1,129},{17,145},{2,130},{18,146},{3,131},{19,147... | collective-permute-start | bytes 1376264 | tf_op jit(solution)/shard_map/ppermute | solution.py:27
  22.5 1.5 convolution_convert_fusion.1
  24.8 33.7 %all_to_all.18 = bf16[16,48,128]{2,1,0:T(8,128)(2,1)S(1)} all-to-all(bf16[16,48,128]{2,1,0:T(8,128)(2,1)S(1)} %pad_maximum_fusion), channel_id=1, replica_groups=mesh['dp'=16,'tensor'=16] {'tensor'}, dimensions={0} | all-to-all | bytes 393216 | tf_op jit(solution)/shard_map/all_to_all | solution.py:272
  58.5 0.8 copy-done.5
  59.4 5.3 %collective-permute-start.9 = (bf16[448,512]{1,0:T(8,128)(2,1)S(1)}, bf16[448,512]{1,0:T(8,128)(2,1)S(1)}, u32[]{:S(2)}, u32[]{:S(2)}) collective-permute-start(bf16[448,512]{1,0:T(8,128)(2,1)S(1)} %slice.29), channel_id=1, source_target_pairs={{0,128},{16,144},{1,129},{17,145},{2,130},{18,146},{3,131},{19,147... | collective-permute-start | bytes 1376264 | tf_op jit(solution)/shard_map/ppermute | solution.py:27
  65.3 2.7 %collective-permute-start.6 = (bf16[768,512]{1,0:T(8,128)(2,1)}, bf16[768,512]{1,0:T(8,128)(2,1)}, u32[]{:S(2)}, u32[]{:S(2)}) collective-permute-start(bf16[768,512]{1,0:T(8,128)(2,1)} %collective-permute-done.3.refs_5_), channel_id=1, source_target_pairs={{0,3},{16,17},{1,0},{17,18},{2,1},{18,19},{3,2},{19,16},{32,35},{4... | collective-permute-start | bytes 2359304 | tf_op jit(solution)/shard_map/ppermute | solution.py:27
  68.0 1.0 collective-permute-start.7
  69.0 16.7 %collective-permute-done.9 = bf16[448,512]{1,0:T(8,128)(2,1)S(1)} collective-permute-done((bf16[448,512]{1,0:T(8,128)(2,1)S(1)}, bf16[448,512]{1,0:T(8,128)(2,1)S(1)}, u32[]{:S(2)}, u32[]{:S(2)}) %collective-permute-start.9) | collective-permute-done | bytes 458784 | tf_op jit(solution)/shard_map/ppermute | solution.py:27
  85.7 0.8 collective-permute-start.8
  86.5 14.7 %collective-permute-done.6.refs_7_ = bf16[768,512]{1,0:T(8,128)(2,1)} collective-permute-done((bf16[768,512]{1,0:T(8,128)(2,1)}, bf16[768,512]{1,0:T(8,128)(2,1)}, u32[]{:S(2)}, u32[]{:S(2)}) %collective-permute-start.6) | collective-permute-done | bytes 786464 | tf_op jit(solution)/shard_map/ppermute | solution.py:27
  101.2 2.4 collective-permute-done.7.refs_8_
  103.6 2.5 %collective-permute-start.10 = (bf16[768,512]{1,0:T(8,128)(2,1)}, bf16[768,512]{1,0:T(8,128)(2,1)}, u32[]{:S(2)}, u32[]{:S(2)}) collective-permute-start(bf16[768,512]{1,0:T(8,128)(2,1)} %collective-permute-done.8.refs_9_), channel_id=1, source_target_pairs={{0,1},{16,19},{1,2},{17,16},{2,3},{18,17},{3,0},{19,18},{32,33},{4... | collective-permute-start | bytes 2359304 | tf_op jit(solution)/shard_map/ppermute | solution.py:27
  106.1 0.8 collective-permute-start.11
  106.9 1.3 collective-permute-start.12
  108.2 1.4 collective-permute-start.13
  109.6 0.7 broadcast_in_dim.77
  110.3 6.1 %all-to-all-start.1 = ((bf16[16,48,128]{2,1,0:T(8,128)(2,1)}), bf16[16,48,128]{2,1,0:T(8,128)(2,1)S(1)}, u32[]{:S(2)}, u32[]{:S(2)}) async-start(bf16[16,48,128]{2,1,0:T(8,128)(2,1)} %broadcast_in_dim.77), calls=%async_computation.1 | async-start | bytes 393216 | tf_op jit(solution)/shard_map/all_to_all | solution.py:294
  116.4 4.1 %fusion.1.refs_12_ = bf16[768,896]{1,0:T(8,128)(2,1)} fusion(bf16[768,896]{1,0:T(8,128)(2,1)} %param.12, bf16[768,896]{1,0:T(8,128)(2,1)} %param.11), kind=kLoop, calls=%fused_computation.6 | loop fusion | flops 7569408 | bytes 4128768 | tf_op jit(solution)/shard_map/convert_element_type | solution.py:302
  120.6 2.9 %fusion.7 = f32[768,64]{0,1:T(8,128)S(1)} fusion(bf16[896,64]{0,1:T(8,128)(2,1)S(1)} %copy-done.8, bf16[768,896]{1,0:T(8,128)(2,1)} %param.12, bf16[768,896]{1,0:T(8,128)(2,1)} %param.11), kind=kOutput, calls=%fused_computation.12 | convolution fusion | flops 93585408 | bytes 3063808 | tf_op jit(solution)/shard_map/dot_general | solution.py:303
  123.5 0.6 collective-permute-done.10.refs_10_
  124.1 19.3 %collective-permute-start.18 = (bf16[4,448,512]{2,1,0:T(8,128)(2,1)S(1)}, bf16[4,448,512]{2,1,0:T(8,128)(2,1)}, u32[]{:S(2)}, u32[]{:S(2)}) collective-permute-start(bf16[4,448,512]{2,1,0:T(8,128)(2,1)S(1)} %bitcast.99), channel_id=1, source_target_pairs={{0,16},{16,0},{1,17},{17,1},{2,18},{18,2},{3,19},{19,3},{32,48},{4... | collective-permute-start | bytes 5505032 | tf_op jit(solution)/shard_map/ppermute | solution.py:27
  143.8 0.6 collective-permute-start.19
  145.2 0.8 pad.8.refs_13_
  146.6 1.2 collective-permute-start.15
  147.8 2.1 collective-permute-start.16
  150.1 2.2 collective-permute-start.17
  152.3 0.9 broadcast_multiply_fusion
  153.6 0.7 pad.9.refs_15_
  154.3 16.9 %shard_map.113.refs_11_ = f32[768,896]{1,0:T(8,128)} custom-call(s32[12]{0:T(128)} %bitcast.112, bf16[768,512]{1,0:T(8,128)(2,1)} %refs_1_.1, bf16[768,512]{1,0:T(8,128)(2,1)} %collective-permute-done.refs_2_, bf16[768,512]{1,0:T(8,128)(2,1)} %collective-permute-done.1.refs_3_, bf16[768,512]{1,0:T(8,128)(2,1)} %collective-permute-done.2.refs_4_, ...), custom_call_target="tpu_custom_call" | custom-call | flops 8455716864 | bytes 23199744 | tf_op jit(solution)/shard_map/pallas_call | solution.py:192
  171.2 0.9 copy-done.3
  172.0 19.0 %shard_map.114 = (f32[2,6,8,128]{3,2,1,0:T(8,128)}, f32[2,6,8,128]{3,2,1,0:T(8,128)}, f32[2,6,8,128]{3,2,1,0:T(8,128)}, f32[2,6,8,128]{3,2,1,0:T(8,128)}) custom-call(s32[5]{0:T(128)} %pad_add_fusion.refs_0_, bf16[768,512]{1,0:T(8,128)(2,1)} %collective-permute-done.13.refs_1_, bf16[768,512]{1,0:T(8,128)(2,1)} %collective-permute-done.15.refs_2_, ...), custom_call_target="tpu_custom_call" | custom-call | flops 2818572288 | bytes 9568256 | tf_op jit(solution)/shard_map/pallas_call | solution.py:192
  191.1 3.2 %collective-permute-start.21 = (f32[2,6,8,128]{3,2,1,0:T(8,128)}, f32[2,6,8,128]{3,2,1,0:T(8,128)S(1)}, u32[]{:S(2)}, u32[]{:S(2)}) collective-permute-start(f32[2,6,8,128]{3,2,1,0:T(8,128)} %get-tuple-element.58), channel_id=1, source_target_pairs={{0,2},{16,18},{1,3},{17,19},{2,0},{18,16},{3,1},{19,17},{32,34},{4... | collective-permute-start | bytes 147464 | tf_op jit(solution)/shard_map/ppermute | solution.py:27
  194.3 2.3 collective-permute-done.20
  197.2 1.4 collective-permute-done.22
  198.6 0.8 add_add_fusion
  199.4 1.0 collective-permute-start.23
  200.4 1.8 collective-permute-start.24
  202.2 1.8 collective-permute-start.25
  204.0 1.1 collective-permute-done.23
  205.4 0.7 collective-permute-done.25
  206.3 4.4 %collective-permute-start.26 = (f32[6,512]{1,0:T(8,128)S(1)}, f32[6,512]{1,0:T(8,128)S(1)}, u32[]{:S(2)}, u32[]{:S(2)}) collective-permute-start(f32[6,512]{1,0:T(8,128)S(1)} %reshape.86), channel_id=1, source_target_pairs={{0,128},{16,144},{1,129},{17,145},{2,130},{18,146},{3,131},{19,147... | collective-permute-start | bytes 36872 | tf_op jit(solution)/shard_map/ppermute | solution.py:27
  210.7 3.3 %collective-permute-done.26 = f32[6,512]{1,0:T(8,128)S(1)} collective-permute-done((f32[6,512]{1,0:T(8,128)S(1)}, f32[6,512]{1,0:T(8,128)S(1)}, u32[]{:S(2)}, u32[]{:S(2)}) %collective-permute-start.26) | collective-permute-done | bytes 12320 | tf_op jit(solution)/shard_map/ppermute | solution.py:27
  214.0 0.8 collective-permute-start.27
  214.8 2.0 collective-permute-start.28
  217.0 0.9 collective-permute-done.27
  217.9 2.3 collective-permute-done.28
  220.2 1.7 collective-permute-done.29
  222.0 1.3 collective-permute-done.30
  224.0 1.6 collective-permute-start.31
  225.6 2.3 collective-permute-start.32
  228.4 0.8 collective-permute-done.31
  229.1 1.8 collective-permute-done.32
  230.9 0.8 collective-permute-done.33
  231.8 0.7 collective-permute-start.34
  232.5 3.2 %collective-permute-start.35 = (f32[6,256]{1,0:T(8,128)S(1)}, f32[6,256]{1,0:T(8,128)S(1)}, u32[]{:S(2)}, u32[]{:S(2)}) collective-permute-start(f32[6,256]{1,0:T(8,128)S(1)} %bitcast.110), channel_id=1, source_target_pairs={{0,8},{16,24},{1,9},{17,25},{2,10},{18,26},{3,11},{19,27},{32,40},... | collective-permute-start | bytes 18440 | tf_op jit(solution)/shard_map/ppermute | solution.py:27
  235.7 1.7 collective-permute-done.34
  237.4 1.9 collective-permute-done.36
  239.3 0.6 fusion.14
  (106 shorter events, 6.4 us)
Async XLA Ops:
  7.2 17.0 %copy-start = (bf16[768,512]{1,0:T(8,128)(2,1)S(1)}, bf16[768,512]{1,0:T(8,128)(2,1)}, u32[]{:S(2)}) copy-start(bf16[768,512]{1,0:T(8,128)(2,1)} %param.10) | copy-start | bytes 2359300
  7.2 52.2 %copy-start.1 = (bf16[896,512]{1,0:T(8,128)(2,1)S(1)}, bf16[896,512]{1,0:T(8,128)(2,1)}, u32[]{:S(2)}) copy-start(bf16[896,512]{1,0:T(8,128)(2,1)} %param.14) | copy-start | bytes 2752516
  7.2 16.9 %copy-start.7 = (bf16[512,64]{0,1:T(8,128)(2,1)S(1)}, bf16[512,64]{0,1:T(8,128)(2,1)}, u32[]{:S(2)}) copy-start(bf16[512,64]{0,1:T(8,128)(2,1)} %param.16) | copy-start | bytes 196612
  7.2 51.3 %all-gather.7.cloned.1.call-start = ((), (), s32[]{:S(2)}) async-start(), calls=%async_computation.2 | async-start | bytes 4587520 | tf_op jit(solution)/shard_map/all_gather | solution.py:259
  7.9 95.6 %all-gather.9.cloned.1.call-start = ((), (), s32[]{:S(2)}) async-start(), calls=%async_computation.3 | async-start | bytes 2293760 | tf_op jit(solution)/shard_map/all_gather | solution.py:259
  8.0 50.5 %collective-permute-start = (bf16[768,512]{1,0:T(8,128)(2,1)}, bf16[768,512]{1,0:T(8,128)(2,1)}, u32[]{:S(2)}, u32[]{:S(2)}) collective-permute-start(bf16[768,512]{1,0:T(8,128)(2,1)} %refs_1_.1), channel_id=1, source_target_pairs={{0,1},{16,19},{1,2},{17,16},{2,3},{18,17},{3,0},{19,18},{32,33},{4... | collective-permute-start | bytes 2359304 | tf_op jit(solution)/shard_map/ppermute | solution.py:27
  9.5 48.9 %collective-permute-start.1 = (bf16[768,512]{1,0:T(8,128)(2,1)}, bf16[768,512]{1,0:T(8,128)(2,1)}, u32[]{:S(2)}, u32[]{:S(2)}) collective-permute-start(bf16[768,512]{1,0:T(8,128)(2,1)} %refs_1_.1), channel_id=1, source_target_pairs={{0,3},{16,17},{1,0},{17,18},{2,1},{18,19},{3,2},{19,16},{32,35},{4... | collective-permute-start | bytes 2359304 | tf_op jit(solution)/shard_map/ppermute | solution.py:27
  11.3 47.2 %collective-permute-start.2 = (bf16[768,512]{1,0:T(8,128)(2,1)}, bf16[768,512]{1,0:T(8,128)(2,1)}, u32[]{:S(2)}, u32[]{:S(2)}) collective-permute-start(bf16[768,512]{1,0:T(8,128)(2,1)} %refs_1_.1), channel_id=1, source_target_pairs={{0,2},{16,18},{1,3},{17,19},{2,0},{18,16},{3,1},{19,17},{32,34},{4... | collective-permute-start | bytes 2359304 | tf_op jit(solution)/shard_map/ppermute | solution.py:27
  13.1 45.4 %collective-permute-start.3 = (bf16[768,512]{1,0:T(8,128)(2,1)}, bf16[768,512]{1,0:T(8,128)(2,1)}, u32[]{:S(2)}, u32[]{:S(2)}) collective-permute-start(bf16[768,512]{1,0:T(8,128)(2,1)} %refs_1_.1), channel_id=1, source_target_pairs={{0,4},{16,28},{1,5},{17,29},{2,6},{18,30},{3,7},{19,31},{32,36},{4... | collective-permute-start | bytes 2359304 | tf_op jit(solution)/shard_map/ppermute | solution.py:27
  16.1 42.4 %collective-permute-start.4 = (bf16[448,512]{1,0:T(8,128)(2,1)S(1)}, bf16[448,512]{1,0:T(8,128)(2,1)S(1)}, u32[]{:S(2)}, u32[]{:S(2)}) collective-permute-start(bf16[448,512]{1,0:T(8,128)(2,1)S(1)} %slice.28), channel_id=1, source_target_pairs={{0,128},{16,144},{1,129},{17,145},{2,130},{18,146},{3,131},{19,147... | collective-permute-start | bytes 1376264 | tf_op jit(solution)/shard_map/ppermute | solution.py:27
  58.5 0.8 copy-start.5
  59.3 84.5 %all-gather.11.cloned.1.call-start = ((), (), s32[]{:S(2)}) async-start(), calls=%async_computation.4 | async-start | bytes 2293760 | tf_op jit(solution)/shard_map/all_gather | solution.py:259
  59.4 61.1 %copy-start.8 = (bf16[896,64]{0,1:T(8,128)(2,1)S(1)}, bf16[896,64]{0,1:T(8,128)(2,1)}, u32[]{:S(2)}) copy-start(bf16[896,64]{0,1:T(8,128)(2,1)} %param.15) | copy-start | bytes 344068
  59.4 26.3 %collective-permute-start.9 = (bf16[448,512]{1,0:T(8,128)(2,1)S(1)}, bf16[448,512]{1,0:T(8,128)(2,1)S(1)}, u32[]{:S(2)}, u32[]{:S(2)}) collective-permute-start(bf16[448,512]{1,0:T(8,128)(2,1)S(1)} %slice.29), channel_id=1, source_target_pairs={{0,128},{16,144},{1,129},{17,145},{2,130},{18,146},{3,131},{19,147... | collective-permute-start | bytes 1376264 | tf_op jit(solution)/shard_map/ppermute | solution.py:27
  64.7 79.1 %collective-permute-start.14 = (bf16[4,896,512]{2,1,0:T(8,128)(2,1)}, bf16[4,896,512]{2,1,0:T(8,128)(2,1)}, u32[]{:S(2)}, u32[]{:S(2)}) collective-permute-start(bf16[4,896,512]{2,1,0:T(8,128)(2,1)} %bitcast.94), channel_id=1, source_target_pairs={{0,16},{16,0},{1,17},{17,1},{2,18},{18,2},{3,19},{19,3},{32,48},{4... | collective-permute-start | bytes 11010056 | tf_op jit(solution)/shard_map/ppermute | solution.py:27
  64.8 21.7 %collective-permute-start.5 = (bf16[768,512]{1,0:T(8,128)(2,1)}, bf16[768,512]{1,0:T(8,128)(2,1)S(1)}, u32[]{:S(2)}, u32[]{:S(2)}) collective-permute-start(bf16[768,512]{1,0:T(8,128)(2,1)} %collective-permute-done.3.refs_5_), channel_id=1, source_target_pairs={{0,1},{16,19},{1,2},{17,16},{2,3},{18,17},{3,0},{19,18},{32,33},{4... | collective-permute-start | bytes 2359304 | tf_op jit(solution)/shard_map/ppermute | solution.py:27
  65.3 35.9 %collective-permute-start.6 = (bf16[768,512]{1,0:T(8,128)(2,1)}, bf16[768,512]{1,0:T(8,128)(2,1)}, u32[]{:S(2)}, u32[]{:S(2)}) collective-permute-start(bf16[768,512]{1,0:T(8,128)(2,1)} %collective-permute-done.3.refs_5_), channel_id=1, source_target_pairs={{0,3},{16,17},{1,0},{17,18},{2,1},{18,19},{3,2},{19,16},{32,35},{4... | collective-permute-start | bytes 2359304 | tf_op jit(solution)/shard_map/ppermute | solution.py:27
  68.0 35.6 %collective-permute-start.7 = (bf16[768,512]{1,0:T(8,128)(2,1)}, bf16[768,512]{1,0:T(8,128)(2,1)}, u32[]{:S(2)}, u32[]{:S(2)}) collective-permute-start(bf16[768,512]{1,0:T(8,128)(2,1)} %collective-permute-done.3.refs_5_), channel_id=1, source_target_pairs={{0,2},{16,18},{1,3},{17,19},{2,0},{18,16},{3,1},{19,17},{32,34},{4... | collective-permute-start | bytes 2359304 | tf_op jit(solution)/shard_map/ppermute | solution.py:27
  85.7 17.9 %copy-start.4 = (bf16[448,512]{1,0:T(8,128)(2,1)}, bf16[448,512]{1,0:T(8,128)(2,1)S(1)}, u32[]{:S(2)}) copy-start(bf16[448,512]{1,0:T(8,128)(2,1)S(1)} %collective-permute-done.9) | copy-start | bytes 1376260
  85.7 17.9 %collective-permute-start.8 = (bf16[768,512]{1,0:T(8,128)(2,1)}, bf16[768,512]{1,0:T(8,128)(2,1)}, u32[]{:S(2)}, u32[]{:S(2)}) collective-permute-start(bf16[768,512]{1,0:T(8,128)(2,1)} %collective-permute-done.3.refs_5_), channel_id=1, source_target_pairs={{0,4},{16,28},{1,5},{17,29},{2,6},{18,30},{3,7},{19,31},{32,36},{4... | collective-permute-start | bytes 2359304 | tf_op jit(solution)/shard_map/ppermute | solution.py:27
  86.5 29.9 %copy-start.13 = (bf16[768,512]{1,0:T(8,128)(2,1)}, bf16[768,512]{1,0:T(8,128)(2,1)S(1)}, u32[]{:S(2)}) copy-start(bf16[768,512]{1,0:T(8,128)(2,1)S(1)} %collective-permute-done.5.refs_6_) | copy-start | bytes 2359300
  103.6 20.5 %collective-permute-start.10 = (bf16[768,512]{1,0:T(8,128)(2,1)}, bf16[768,512]{1,0:T(8,128)(2,1)}, u32[]{:S(2)}, u32[]{:S(2)}) collective-permute-start(bf16[768,512]{1,0:T(8,128)(2,1)} %collective-permute-done.8.refs_9_), channel_id=1, source_target_pairs={{0,1},{16,19},{1,2},{17,16},{2,3},{18,17},{3,0},{19,18},{32,33},{4... | collective-permute-start | bytes 2359304 | tf_op jit(solution)/shard_map/ppermute | solution.py:27
  106.1 37.7 %collective-permute-start.11 = (bf16[768,512]{1,0:T(8,128)(2,1)}, bf16[768,512]{1,0:T(8,128)(2,1)}, u32[]{:S(2)}, u32[]{:S(2)}) collective-permute-start(bf16[768,512]{1,0:T(8,128)(2,1)} %collective-permute-done.8.refs_9_), channel_id=1, source_target_pairs={{0,3},{16,17},{1,0},{17,18},{2,1},{18,19},{3,2},{19,16},{32,35},{4... | collective-permute-start | bytes 2359304 | tf_op jit(solution)/shard_map/ppermute | solution.py:27
  106.9 36.9 %collective-permute-start.12 = (bf16[768,512]{1,0:T(8,128)(2,1)}, bf16[768,512]{1,0:T(8,128)(2,1)}, u32[]{:S(2)}, u32[]{:S(2)}) collective-permute-start(bf16[768,512]{1,0:T(8,128)(2,1)} %collective-permute-done.8.refs_9_), channel_id=1, source_target_pairs={{0,2},{16,18},{1,3},{17,19},{2,0},{18,16},{3,1},{19,17},{32,34},{4... | collective-permute-start | bytes 2359304 | tf_op jit(solution)/shard_map/ppermute | solution.py:27
  108.2 35.6 %collective-permute-start.13 = (bf16[768,512]{1,0:T(8,128)(2,1)}, bf16[768,512]{1,0:T(8,128)(2,1)}, u32[]{:S(2)}, u32[]{:S(2)}) collective-permute-start(bf16[768,512]{1,0:T(8,128)(2,1)} %collective-permute-done.8.refs_9_), channel_id=1, source_target_pairs={{0,4},{16,28},{1,5},{17,29},{2,6},{18,30},{3,7},{19,31},{32,36},{4... | collective-permute-start | bytes 2359304 | tf_op jit(solution)/shard_map/ppermute | solution.py:27
  110.3 33.5 %all-to-all-start.1 = ((bf16[16,48,128]{2,1,0:T(8,128)(2,1)}), bf16[16,48,128]{2,1,0:T(8,128)(2,1)S(1)}, u32[]{:S(2)}, u32[]{:S(2)}) async-start(bf16[16,48,128]{2,1,0:T(8,128)(2,1)} %broadcast_in_dim.77), calls=%async_computation.1 | async-start | bytes 393216 | tf_op jit(solution)/shard_map/all_to_all | solution.py:294
  120.6 3.5 %copy-start.2 = (bf16[1792,512]{1,0:T(8,128)(2,1)S(1)}, bf16[1792,512]{1,0:T(8,128)(2,1)}, u32[]{:S(2)}) copy-start(bf16[1792,512]{1,0:T(8,128)(2,1)} %all-gather.9.cloned.1.call-done) | copy-start | bytes 5505028
  120.6 24.1 %copy-start.10 = (s32[6,2]{0,1:T(2,128)S(1)}, s32[6,2]{0,1:T(2,128)}, u32[]{:S(2)}) copy-start(s32[6,2]{0,1:T(2,128)} %param.18) | copy-start | bytes 148
  120.6 24.2 %copy-start.11 = (s32[6]{0:T(128)S(1)}, s32[6]{0:T(128)}, u32[]{:S(2)}) copy-start(s32[6]{0:T(128)} %param.19) | copy-start | bytes 76
  124.1 30.2 %collective-permute-start.18 = (bf16[4,448,512]{2,1,0:T(8,128)(2,1)S(1)}, bf16[4,448,512]{2,1,0:T(8,128)(2,1)}, u32[]{:S(2)}, u32[]{:S(2)}) collective-permute-start(bf16[4,448,512]{2,1,0:T(8,128)(2,1)S(1)} %bitcast.99), channel_id=1, source_target_pairs={{0,16},{16,0},{1,17},{17,1},{2,18},{18,2},{3,19},{19,3},{32,48},{4... | collective-permute-start | bytes 5505032 | tf_op jit(solution)/shard_map/ppermute | solution.py:27
  143.8 10.4 %collective-permute-start.19 = (bf16[4,448,512]{2,1,0:T(8,128)(2,1)}, bf16[4,448,512]{2,1,0:T(8,128)(2,1)}, u32[]{:S(2)}, u32[]{:S(2)}) collective-permute-start(bf16[4,448,512]{2,1,0:T(8,128)(2,1)} %bitcast.100), channel_id=1, source_target_pairs={{0,16},{16,0},{1,17},{17,1},{2,18},{18,2},{3,19},{19,3},{32,48},{4... | collective-permute-start | bytes 5505032 | tf_op jit(solution)/shard_map/ppermute | solution.py:27
  145.1 9.1 %copy-start.12 = (s32[16]{0:T(128)}, s32[16]{0:T(128)S(1)}, u32[]{:S(2)}) copy-start(s32[16]{0:T(128)S(1)} %fusion.16) | copy-start | bytes 196
  146.6 24.5 %collective-permute-start.15 = (bf16[768,512]{1,0:T(8,128)(2,1)}, bf16[768,512]{1,0:T(8,128)(2,1)}, u32[]{:S(2)}, u32[]{:S(2)}) collective-permute-start(bf16[768,512]{1,0:T(8,128)(2,1)} %collective-permute-done.13.refs_1_), channel_id=1, source_target_pairs={{0,1},{16,19},{1,2},{17,16},{2,3},{18,17},{3,0},{19,18},{32,33},{4... | collective-permute-start | bytes 2359304 | tf_op jit(solution)/shard_map/ppermute | solution.py:27
  147.8 23.3 %collective-permute-start.16 = (bf16[768,512]{1,0:T(8,128)(2,1)}, bf16[768,512]{1,0:T(8,128)(2,1)}, u32[]{:S(2)}, u32[]{:S(2)}) collective-permute-start(bf16[768,512]{1,0:T(8,128)(2,1)} %collective-permute-done.13.refs_1_), channel_id=1, source_target_pairs={{0,3},{16,17},{1,0},{17,18},{2,1},{18,19},{3,2},{19,16},{32,35},{4... | collective-permute-start | bytes 2359304 | tf_op jit(solution)/shard_map/ppermute | solution.py:27
  150.1 21.0 %collective-permute-start.17 = (bf16[768,512]{1,0:T(8,128)(2,1)}, bf16[768,512]{1,0:T(8,128)(2,1)S(1)}, u32[]{:S(2)}, u32[]{:S(2)}) collective-permute-start(bf16[768,512]{1,0:T(8,128)(2,1)} %collective-permute-done.12.refs_12_), channel_id=1, source_target_pairs={{0,4},{16,28},{1,5},{17,29},{2,6},{18,30},{3,7},{19,31},{32,36},{4... | collective-permute-start | bytes 2359304 | tf_op jit(solution)/shard_map/ppermute | solution.py:27
  171.1 0.9 copy-start.3
  191.0 32.4 %copy-start.6 = (bf16[256,512]{1,0:T(8,128)(2,1)S(1)}, bf16[256,512]{1,0:T(8,128)(2,1)}, u32[]{:S(2)}) copy-start(bf16[256,512]{1,0:T(8,128)(2,1)} %param.17) | copy-start | bytes 786436
  191.0 5.6 %collective-permute-start.20 = (f32[2,6,8,128]{3,2,1,0:T(8,128)}, f32[2,6,8,128]{3,2,1,0:T(8,128)S(1)}, u32[]{:S(2)}, u32[]{:S(2)}) collective-permute-start(f32[2,6,8,128]{3,2,1,0:T(8,128)} %get-tuple-element.57), channel_id=1, source_target_pairs={{0,1},{16,17},{1,2},{17,18},{2,3},{18,19},{3,0},{19,16},{32,33},{4... | collective-permute-start | bytes 147464 | tf_op jit(solution)/shard_map/ppermute | solution.py:27
  191.1 6.1 %collective-permute-start.21 = (f32[2,6,8,128]{3,2,1,0:T(8,128)}, f32[2,6,8,128]{3,2,1,0:T(8,128)S(1)}, u32[]{:S(2)}, u32[]{:S(2)}) collective-permute-start(f32[2,6,8,128]{3,2,1,0:T(8,128)} %get-tuple-element.58), channel_id=1, source_target_pairs={{0,2},{16,18},{1,3},{17,19},{2,0},{18,16},{3,1},{19,17},{32,34},{4... | collective-permute-start | bytes 147464 | tf_op jit(solution)/shard_map/ppermute | solution.py:27
  194.3 4.3 %collective-permute-start.22 = (f32[2,6,8,128]{3,2,1,0:T(8,128)}, f32[2,6,8,128]{3,2,1,0:T(8,128)S(1)}, u32[]{:S(2)}, u32[]{:S(2)}) collective-permute-start(f32[2,6,8,128]{3,2,1,0:T(8,128)} %get-tuple-element.59), channel_id=1, source_target_pairs={{0,3},{16,19},{1,0},{17,16},{2,1},{18,17},{3,2},{19,18},{32,35},{4... | collective-permute-start | bytes 147464 | tf_op jit(solution)/shard_map/ppermute | solution.py:27
  199.4 5.7 %collective-permute-start.23 = (f32[6,8,128]{2,1,0:T(8,128)S(1)}, f32[6,8,128]{2,1,0:T(8,128)S(1)}, u32[]{:S(2)}, u32[]{:S(2)}) collective-permute-start(f32[6,8,128]{2,1,0:T(8,128)S(1)} %get-tuple-element.63), channel_id=1, source_target_pairs={{0,4},{16,20},{1,5},{17,21},{2,6},{18,22},{3,7},{19,23},{32,36},{4... | collective-permute-start | bytes 73736 | tf_op jit(solution)/shard_map/ppermute | solution.py:27
  200.4 5.0 %collective-permute-start.24 = (f32[6,8,128]{2,1,0:T(8,128)S(1)}, f32[6,8,128]{2,1,0:T(8,128)S(1)}, u32[]{:S(2)}, u32[]{:S(2)}) collective-permute-start(f32[6,8,128]{2,1,0:T(8,128)S(1)} %get-tuple-element.65), channel_id=1, source_target_pairs={{0,8},{16,24},{1,9},{17,25},{2,10},{18,26},{3,11},{19,27},{32,40},... | collective-permute-start | bytes 73736 | tf_op jit(solution)/shard_map/ppermute | solution.py:27
  202.2 3.8 %collective-permute-start.25 = (f32[6,8,128]{2,1,0:T(8,128)S(1)}, f32[6,8,128]{2,1,0:T(8,128)S(1)}, u32[]{:S(2)}, u32[]{:S(2)}) collective-permute-start(f32[6,8,128]{2,1,0:T(8,128)S(1)} %get-tuple-element.64), channel_id=1, source_target_pairs={{0,12},{16,28},{1,13},{17,29},{2,14},{18,30},{3,15},{19,31},{32,44... | collective-permute-start | bytes 73736 | tf_op jit(solution)/shard_map/ppermute | solution.py:27
  206.3 33.6 %copy-start.9 = (f32[6,512]{1,0:T(8,128)}, f32[6,512]{1,0:T(8,128)S(1)}, u32[]{:S(2)}) copy-start(f32[6,512]{1,0:T(8,128)S(1)} %reshape.86) | copy-start | bytes 36868
  206.3 7.7 %collective-permute-start.26 = (f32[6,512]{1,0:T(8,128)S(1)}, f32[6,512]{1,0:T(8,128)S(1)}, u32[]{:S(2)}, u32[]{:S(2)}) collective-permute-start(f32[6,512]{1,0:T(8,128)S(1)} %reshape.86), channel_id=1, source_target_pairs={{0,128},{16,144},{1,129},{17,145},{2,130},{18,146},{3,131},{19,147... | collective-permute-start | bytes 36872 | tf_op jit(solution)/shard_map/ppermute | solution.py:27
  214.0 3.9 %collective-permute-start.27 = (f32[2,6,512]{2,1,0:T(8,128)S(1)}, f32[2,6,512]{2,1,0:T(8,128)S(1)}, u32[]{:S(2)}, u32[]{:S(2)}) collective-permute-start(f32[2,6,512]{2,1,0:T(8,128)S(1)} %bitcast_dynamic-update-slice_fusion.6), channel_id=1, source_target_pairs={{0,32},{16,48},{1,33},{17,49},{2,34},{18,50},{3,35},{19,51},{32,64... | collective-permute-start | bytes 73736 | tf_op jit(solution)/shard_map/ppermute | solution.py:27
  214.8 5.4 %collective-permute-start.28 = (f32[2,6,512]{2,1,0:T(8,128)S(1)}, f32[2,6,512]{2,1,0:T(8,128)S(1)}, u32[]{:S(2)}, u32[]{:S(2)}) collective-permute-start(f32[2,6,512]{2,1,0:T(8,128)S(1)} %bitcast_dynamic-update-slice_fusion.6), channel_id=1, source_target_pairs={{0,64},{16,80},{1,65},{17,81},{2,66},{18,82},{3,67},{19,83},{32,96... | collective-permute-start | bytes 73736 | tf_op jit(solution)/shard_map/ppermute | solution.py:27
  216.9 5.1 %collective-permute-start.29 = (f32[2,6,512]{2,1,0:T(8,128)S(1)}, f32[2,6,512]{2,1,0:T(8,128)S(1)}, u32[]{:S(2)}, u32[]{:S(2)}) collective-permute-start(f32[2,6,512]{2,1,0:T(8,128)S(1)} %bitcast_dynamic-update-slice_fusion.6), channel_id=1, source_target_pairs={{0,96},{16,112},{1,97},{17,113},{2,98},{18,114},{3,99},{19,115},{3... | collective-permute-start | bytes 73736 | tf_op jit(solution)/shard_map/ppermute | solution.py:27
  222.0 1.3 collective-permute-start.30
  224.0 5.1 %collective-permute-start.31 = (f32[4,6,256]{2,0,1:T(4,128)S(1)}, f32[4,6,256]{2,0,1:T(4,128)S(1)}, u32[]{:S(2)}, u32[]{:S(2)}) collective-permute-start(f32[4,6,256]{2,0,1:T(4,128)S(1)} %get-tuple-element.60), channel_id=1, source_target_pairs={{0,1},{16,17},{1,2},{17,18},{2,3},{18,19},{3,0},{19,16},{32,33},{4... | collective-permute-start | bytes 73736 | tf_op jit(solution)/shard_map/ppermute | solution.py:27
  225.6 5.3 %collective-permute-start.32 = (f32[4,6,256]{2,0,1:T(4,128)S(1)}, f32[4,6,256]{2,0,1:T(4,128)S(1)}, u32[]{:S(2)}, u32[]{:S(2)}) collective-permute-start(f32[4,6,256]{2,0,1:T(4,128)S(1)} %get-tuple-element.62), channel_id=1, source_target_pairs={{0,2},{16,18},{1,3},{17,19},{2,0},{18,16},{3,1},{19,17},{32,34},{4... | collective-permute-start | bytes 73736 | tf_op jit(solution)/shard_map/ppermute | solution.py:27
  227.9 3.8 %collective-permute-start.33 = (f32[4,6,256]{2,0,1:T(4,128)S(1)}, f32[4,6,256]{2,0,1:T(4,128)S(1)}, u32[]{:S(2)}, u32[]{:S(2)}) collective-permute-start(f32[4,6,256]{2,0,1:T(4,128)S(1)} %get-tuple-element.61), channel_id=1, source_target_pairs={{0,3},{16,19},{1,0},{17,16},{2,1},{18,17},{3,2},{19,18},{32,35},{4... | collective-permute-start | bytes 73736 | tf_op jit(solution)/shard_map/ppermute | solution.py:27
  231.8 5.6 %collective-permute-start.34 = (f32[6,256]{1,0:T(8,128)S(1)}, f32[6,256]{1,0:T(8,128)S(1)}, u32[]{:S(2)}, u32[]{:S(2)}) collective-permute-start(f32[6,256]{1,0:T(8,128)S(1)} %bitcast.109), channel_id=1, source_target_pairs={{0,4},{16,20},{1,5},{17,21},{2,6},{18,22},{3,7},{19,23},{32,36},{4... | collective-permute-start | bytes 18440 | tf_op jit(solution)/shard_map/ppermute | solution.py:27
  232.5 4.9 %collective-permute-start.35 = (f32[6,256]{1,0:T(8,128)S(1)}, f32[6,256]{1,0:T(8,128)S(1)}, u32[]{:S(2)}, u32[]{:S(2)}) collective-permute-start(f32[6,256]{1,0:T(8,128)S(1)} %bitcast.110), channel_id=1, source_target_pairs={{0,8},{16,24},{1,9},{17,25},{2,10},{18,26},{3,11},{19,27},{32,40},... | collective-permute-start | bytes 18440 | tf_op jit(solution)/shard_map/ppermute | solution.py:27
  235.7 3.7 %collective-permute-start.36 = (f32[6,256]{1,0:T(8,128)S(1)}, f32[6,256]{1,0:T(8,128)S(1)}, u32[]{:S(2)}, u32[]{:S(2)}) collective-permute-start(f32[6,256]{1,0:T(8,128)S(1)} %bitcast.111), channel_id=1, source_target_pairs={{0,12},{16,28},{1,13},{17,29},{2,14},{18,30},{3,15},{19,31},{32,44... | collective-permute-start | bytes 18440 | tf_op jit(solution)/shard_map/ppermute | solution.py:27
Sparse Core Ops, SparseCore 0:
  9.8 47.2 all-gather.6
  59.4 31.2 all-gather.8
  103.7 30.6 all-gather.10
where the time goes:
time: 251 us; the launch traced here: 247 us
  starting transfers between devices  84.9 us (34%)
  waiting for transfers between devices  58.4 us (23%)
  Pallas kernels  35.8 us (14%)
  blocking collectives  33.7 us (13%)
  between operations  14.4 us (6%)
  other arithmetic  7.44 us (3%)
  local copies, waits for them, and re-layouts  6.52 us (3%)
  matrix products  5.47 us (2%)
    ppermute x37, starting transfers between devices, move(): return lax.ppermute(value, AXES, pairs)  78.7 us
    ppermute x37, waiting for transfers between devices, move(): return lax.ppermute(value, AXES, pairs)  57.2 us
    pallas_call x2, Pallas kernels, products(): pl.pallas_call(lambda *refs: product_kernel(count, last, *refs), out_shap...  35.8 us
    all_to_all x1, blocking collectives, local(): dealt = lax.all_to_all(terms, 'tensor', 0, 0, tiled=True)  33.7 us
    all_to_all x1, starting transfers between devices, local(): lax.all_to_all(jnp.broadcast_to(mine, (16, sixteenth, 2 * sk)).reshape(to...  6.14 us
  transfers between devices with their start and end apart: 41, of which 21 were waited for; matrix products, arithmetic and copies ran while one was open for 6% of the time, Pallas kernels for 7%

commit v1 on v0

--- a/solution.py
+++ b/solution.py
@@ -53,6 +53,10 @@
 
 def line_z_both(x, y, z, c):
     return line_z(side(c))(x, y, z, c)
+
+
+def across_both(x, y, z, c):
+    return shift_x(2)(x, y, z, c) if c == 0 else line_z_both(x, y, z, c)
 
 
 def swap_core(x, y, z, c):
@@ -270,52 +274,52 @@
         axis=1,
     ).astype(BF16)
     dealt = lax.all_to_all(terms, "tensor", 0, 0, tiled=True)
+    hop1 = move(grad_out, line_z_both)
     ahead0 = move(grad_out, ring_x(1))
     behind0 = move(grad_out, ring_x(-1))
     across0 = move(grad_out, shift_x(2))
-    hop1 = move(grad_out, line_z_both)
     far_a = move(down_weight[:mid], swap_half)
-    ahead0, behind0, across0, hop1, far_a, weight_rows, dealt, near_own = turn(
-        ahead0, behind0, across0, hop1, far_a, down_weight, dealt, near_own
+    hop1, ahead0, behind0, across0, far_a, weight_rows, dealt, near_own = turn(
+        hop1, ahead0, behind0, across0, far_a, down_weight, dealt, near_own
     )
 
     far_own_a = along_y(far_a)
     mine = dealt.reshape(16, sixteenth, 2 * sk).astype(F32).sum(axis=0).astype(BF16)
+    full = lax.all_to_all(
+        jnp.broadcast_to(mine, (16, sixteenth, 2 * sk)).reshape(tok_rows, 2 * sk),
+        "tensor", 0, 0, tiled=True,
+    )
+    hop2 = move(hop1, line_z_both)
     ahead1 = move(hop1, ring_x(1))
     behind1 = move(hop1, ring_x(-1))
     across1 = move(hop1, shift_x(2))
-    hop2 = move(hop1, line_z_both)
     far_b = move(weight_rows[mid:], swap_half)
-    ahead1, behind1, across1, hop2, far_b, far_own_a, mine, gate_saved = turn(
-        ahead1, behind1, across1, hop2, far_b, far_own_a, mine, gate_saved
+    hop2, ahead1, behind1, across1, far_b, far_own_a, full, near_own, gate_saved = turn(
+        hop2, ahead1, behind1, across1, far_b, far_own_a, full, near_own, gate_saved
     )
 
     far_own_b = along_y(far_b)
-    full = lax.all_to_all(
-        jnp.broadcast_to(mine, (16, sixteenth, 2 * sk)).reshape(tok_rows, 2 * sk),
-        "tensor", 0, 0, tiled=True,
-    )
     gate32 = gate_saved.astype(F32)
     up32 = up_saved.astype(F32)
     sig = jax.nn.sigmoid(gate32)
     hidden = (gate32 * sig * up32).astype(BF16)
     slope = (up32 * sig * (1.0 + gate32 * (1.0 - sig))).astype(BF16)
     a = jnp.dot(hidden, hidden_proj, preferred_element_type=F32)
+    hop3 = move(hop2, line_z_both)
     ahead2 = move(hop2, ring_x(1))
     behind2 = move(hop2, ring_x(-1))
-    across2 = move(hop2, shift_x(2))
-    hop3 = move(hop2, line_z_both)
+    across2 = move(jnp.where(c == 0, hop2, across1), across_both)
     near_other = move(near_own, swap_core)
-    ahead2, behind2, across2, hop3, near_other, full, slope, a, far_own_b = turn(
-        ahead2, behind2, across2, hop3, near_other, full, slope, a, far_own_b
+    hop3, ahead2, behind2, across2, near_other, far_own_a, far_own_b, slope, a = turn(
+        hop3, ahead2, behind2, across2, near_other, far_own_a, far_own_b, slope, a
     )
     full = full.astype(F32)
 
     ahead3 = move(hop3, ring_x(1))
     behind3 = move(hop3, ring_x(-1))
     across3 = move(across2, line_z_both)
+    far_other_a = move(far_own_a, swap_core)
     far_other_b = move(far_own_b, swap_core)
-    far_other_a = move(far_own_a, swap_core)
     pieces = [
         grad_out, ahead0, behind0, across0,
         hop1, ahead1, behind1, across1,

time: 251 us -> 243 us (0.968)
  blocking collectives: 33.7 us -> 63.4 us
  starting transfers between devices: 84.9 us -> 60.6 us
  waiting for transfers between devices: 58.4 us -> 44.3 us
    all_to_all x0 -> x1, blocking collectives: none -> 33.2 us  [local(): lax.all_to_all(jnp.broadcast_to(mine, (16, sixteenth, 2 * sk)).reshape(to...]
    ppermute x37, starting transfers between devices: 78.7 us -> 60.5 us  [move(): return lax.ppermute(value, AXES, pairs)]
    ppermute x37, waiting for transfers between devices: 57.2 us -> 42.2 us  [move(): return lax.ppermute(value, AXES, pairs)]
    all_to_all x1 -> x0, starting transfers between devices: 6.14 us -> none  [local(): lax.all_to_all(jnp.broadcast_to(mine, (16, sixteenth, 2 * sk)).reshape(to...]
    all_to_all x1, blocking collectives: 33.7 us -> 30.2 us  [local(): dealt = lax.all_to_all(terms, 'tensor', 0, 0, tiled=True)]
  transfers between devices with their start and end apart: 41 -> 40, of which waited for: 21 -> 19; matrix products, arithmetic and copies ran while one was open for 6% -> 6% of each run, Pallas kernels for 7% -> 7%
where the time goes in v1:
time: 243 us; the launch traced here: 239 us
  blocking collectives  63.4 us (26%)
  starting transfers between devices  60.6 us (25%)
  waiting for transfers between devices  44.3 us (18%)
  Pallas kernels  35.8 us (15%)
  between operations  14.5 us (6%)
  local copies, waits for them, and re-layouts  8.25 us (3%)
  other arithmetic  6.82 us (3%)
  matrix products  4.95 us (2%)
    ppermute x37, starting transfers between devices, move(): return lax.ppermute(value, AXES, pairs)  60.5 us
    ppermute x37, waiting for transfers between devices, move(): return lax.ppermute(value, AXES, pairs)  42.2 us
    pallas_call x2, Pallas kernels, products(): pl.pallas_call(lambda *refs: product_kernel(count, last, *refs), out_shap...  35.8 us
    all_to_all x1, blocking collectives, local(): lax.all_to_all(jnp.broadcast_to(mine, (16, sixteenth, 2 * sk)).reshape(to...  33.2 us
    all_to_all x1, blocking collectives, local(): dealt = lax.all_to_all(terms, 'tensor', 0, 0, tiled=True)  30.2 us
  transfers between devices with their start and end apart: 40, of which 19 were waited for; matrix products, arithmetic and copies ran while one was open for 6% of the time, Pallas kernels for 7%

profile of v1, /device:TPU:24, one launch (start us, length us, event | category | flops | bytes accessed | tf_op | source)
XLA Modules:
  0.0 238.7 jit_solution(5059566973281134330)
XLA Ops:
  7.2 0.7 all-gather.7.cloned.1.call-update
  8.0 2.0 collective-permute-start
  10.0 1.5 collective-permute-start.1
  11.5 1.7 collective-permute-start.2
  13.2 1.8 collective-permute-start.3
  15.0 1.8 slice.28
  16.9 6.3 %collective-permute-start.4 = (bf16[448,512]{1,0:T(8,128)(2,1)}, bf16[448,512]{1,0:T(8,128)(2,1)}, u32[]{:S(2)}, u32[]{:S(2)}) collective-permute-start(bf16[448,512]{1,0:T(8,128)(2,1)} %slice.28), channel_id=1, source_target_pairs={{0,128},{16,144},{1,129},{17,145},{2,130},{18,146},{3,131},{19,147... | collective-permute-start | bytes 1376264 | tf_op jit(solution)/shard_map/ppermute | solution.py:27
  23.1 1.5 convolution_convert_fusion.1
  25.6 30.2 %all_to_all.18 = bf16[16,48,128]{2,1,0:T(8,128)(2,1)S(1)} all-to-all(bf16[16,48,128]{2,1,0:T(8,128)(2,1)S(1)} %pad_maximum_fusion), channel_id=1, replica_groups=mesh['dp'=16,'tensor'=16] {'tensor'}, dimensions={0} | all-to-all | bytes 393216 | tf_op jit(solution)/shard_map/all_to_all | solution.py:276
  55.8 1.3 all-gather.7.cloned.1.call-done
  57.2 1.8 collective-permute-start.5
  59.0 1.5 collective-permute-start.6
  60.5 1.8 collective-permute-start.7
  62.3 1.8 collective-permute-start.8
  64.1 0.8 slice.29
  64.9 4.8 %collective-permute-start.9 = (bf16[448,512]{1,0:T(8,128)(2,1)}, bf16[448,512]{1,0:T(8,128)(2,1)S(1)}, u32[]{:S(2)}, u32[]{:S(2)}) collective-permute-start(bf16[448,512]{1,0:T(8,128)(2,1)} %slice.29), channel_id=1, source_target_pairs={{0,128},{16,144},{1,129},{17,145},{2,130},{18,146},{3,131},{19,147... | collective-permute-start | bytes 1376264 | tf_op jit(solution)/shard_map/ppermute | solution.py:27
  69.8 33.2 %all_to_all.19 = bf16[16,48,128]{2,1,0:T(8,128)(2,1)S(1)} all-to-all(bf16[16,48,128]{2,1,0:T(8,128)(2,1)S(1)} %broadcast_in_dim.77), channel_id=1, replica_groups=mesh['dp'=16,'tensor'=16] {'tensor'}, dimensions={0} | all-to-all | bytes 393216 | tf_op jit(solution)/shard_map/all_to_all | solution.py:288
  103.2 0.7 copy-done.7
  104.0 1.7 collective-permute-start.11
  105.7 1.6 collective-permute-start.12
  107.3 1.2 broadcast_select_fusion
  108.6 2.1 collective-permute-start.13
  110.7 2.3 fusion.7
  113.1 2.3 fusion.1.refs_12_
  115.3 19.9 %collective-permute-done.13.refs_12_ = bf16[768,512]{1,0:T(8,128)(2,1)S(1)} collective-permute-done((bf16[768,512]{1,0:T(8,128)(2,1)S(1)}, bf16[768,512]{1,0:T(8,128)(2,1)S(1)}, u32[]{:S(2)}, u32[]{:S(2)}) %collective-permute-start.13) | collective-permute-done | bytes 786464 | tf_op jit(solution)/shard_map/ppermute | solution.py:27
  135.2 0.9 copy-done.15
  136.3 0.5 collective-permute-start.19
  137.5 0.8 pad.8.refs_13_
  138.4 0.6 pad_add_fusion.refs_0_
  138.9 0.8 collective-permute-start.15
  139.7 2.5 %collective-permute-start.16 = (bf16[768,512]{1,0:T(8,128)(2,1)}, bf16[768,512]{1,0:T(8,128)(2,1)}, u32[]{:S(2)}, u32[]{:S(2)}) collective-permute-start(bf16[768,512]{1,0:T(8,128)(2,1)} %collective-permute-done.10.refs_1_), channel_id=1, source_target_pairs={{0,3},{16,17},{1,0},{17,18},{2,1},{18,19},{3,2},{19,16},{32,35},{4... | collective-permute-start | bytes 2359304 | tf_op jit(solution)/shard_map/ppermute | solution.py:27
  142.3 0.6 collective-permute-start.17
  142.9 0.9 broadcast_multiply_fusion
  144.2 0.7 pad.9.refs_15_
  144.9 16.9 %shard_map.113.refs_11_ = f32[768,896]{1,0:T(8,128)} custom-call(s32[12]{0:T(128)} %bitcast.112, bf16[768,512]{1,0:T(8,128)(2,1)} %refs_1_.1, bf16[768,512]{1,0:T(8,128)(2,1)} %collective-permute-done.1.refs_2_, bf16[768,512]{1,0:T(8,128)(2,1)} %collective-permute-done.2.refs_3_, bf16[768,512]{1,0:T(8,128)(2,1)} %collective-permute-done.3.refs_4_, ...), custom_call_target="tpu_custom_call" | custom-call | flops 8455716864 | bytes 23199744 | tf_op jit(solution)/shard_map/pallas_call | solution.py:196
  161.9 0.9 copy-done.6
  162.8 19.0 %shard_map.114 = (f32[2,6,8,128]{3,2,1,0:T(8,128)}, f32[2,6,8,128]{3,2,1,0:T(8,128)}, f32[2,6,8,128]{3,2,1,0:T(8,128)}, f32[2,6,8,128]{3,2,1,0:T(8,128)}) custom-call(s32[5]{0:T(128)} %pad_add_fusion.refs_0_, bf16[768,512]{1,0:T(8,128)(2,1)} %collective-permute-done.10.refs_1_, bf16[768,512]{1,0:T(8,128)(2,1)} %collective-permute-done.15.refs_2_, ...), custom_call_target="tpu_custom_call" | custom-call | flops 2818572288 | bytes 9568256 | tf_op jit(solution)/shard_map/pallas_call | solution.py:196
  182.1 2.7 %collective-permute-start.21 = (f32[2,6,8,128]{3,2,1,0:T(8,128)}, f32[2,6,8,128]{3,2,1,0:T(8,128)S(1)}, u32[]{:S(2)}, u32[]{:S(2)}) collective-permute-start(f32[2,6,8,128]{3,2,1,0:T(8,128)} %get-tuple-element.60), channel_id=1, source_target_pairs={{0,2},{16,18},{1,3},{17,19},{2,0},{18,16},{3,1},{19,17},{32,34},{4... | collective-permute-start | bytes 147464 | tf_op jit(solution)/shard_map/ppermute | solution.py:27
  184.9 1.0 collective-permute-start.22
  185.9 2.5 %collective-permute-done.20 = f32[2,6,8,128]{3,2,1,0:T(8,128)S(1)} collective-permute-done((f32[2,6,8,128]{3,2,1,0:T(8,128)}, f32[2,6,8,128]{3,2,1,0:T(8,128)S(1)}, u32[]{:S(2)}, u32[]{:S(2)}) %collective-permute-start.20) | collective-permute-done | bytes 49184 | tf_op jit(solution)/shard_map/ppermute | solution.py:27
  188.4 0.8 collective-permute-done.22
  189.2 0.8 add_add_fusion
  190.0 1.6 collective-permute-start.23
  191.7 1.7 collective-permute-start.24
  193.3 1.3 collective-permute-start.25
  194.6 1.2 collective-permute-done.23
  195.8 0.8 collective-permute-done.24
  197.4 4.3 %collective-permute-start.26 = (f32[6,512]{1,0:T(8,128)S(1)}, f32[6,512]{1,0:T(8,128)S(1)}, u32[]{:S(2)}, u32[]{:S(2)}) collective-permute-start(f32[6,512]{1,0:T(8,128)S(1)} %reshape.86), channel_id=1, source_target_pairs={{0,128},{16,144},{1,129},{17,145},{2,130},{18,146},{3,131},{19,147... | collective-permute-start | bytes 36872 | tf_op jit(solution)/shard_map/ppermute | solution.py:27
  201.7 3.4 %collective-permute-done.26 = f32[6,512]{1,0:T(8,128)S(1)} collective-permute-done((f32[6,512]{1,0:T(8,128)S(1)}, f32[6,512]{1,0:T(8,128)S(1)}, u32[]{:S(2)}, u32[]{:S(2)}) %collective-permute-start.26) | collective-permute-done | bytes 12320 | tf_op jit(solution)/shard_map/ppermute | solution.py:27
  205.1 2.2 collective-permute-start.27
  207.3 1.4 collective-permute-start.28
  209.0 3.7 %collective-permute-done.28 = f32[2,6,512]{2,1,0:T(8,128)S(1)} collective-permute-done((f32[2,6,512]{2,1,0:T(8,128)S(1)}, f32[2,6,512]{2,1,0:T(8,128)S(1)}, u32[]{:S(2)}, u32[]{:S(2)}) %collective-permute-start.28) | collective-permute-done | bytes 24608 | tf_op jit(solution)/shard_map/ppermute | solution.py:27
  212.7 1.1 collective-permute-done.29
  213.9 1.3 collective-permute-done.30
  215.8 1.6 collective-permute-start.31
  217.4 2.3 collective-permute-start.32
  220.2 0.8 collective-permute-done.31
  220.9 1.8 collective-permute-done.32
  222.7 0.8 collective-permute-done.33
  223.6 1.4 collective-permute-start.34
  225.0 2.7 %collective-permute-start.35 = (f32[6,256]{1,0:T(8,128)S(1)}, f32[6,256]{1,0:T(8,128)S(1)}, u32[]{:S(2)}, u32[]{:S(2)}) collective-permute-start(f32[6,256]{1,0:T(8,128)S(1)} %bitcast.110), channel_id=1, source_target_pairs={{0,8},{16,24},{1,9},{17,25},{2,10},{18,26},{3,11},{19,27},{32,40},... | collective-permute-start | bytes 18440 | tf_op jit(solution)/shard_map/ppermute | solution.py:27
  227.9 1.2 collective-permute-done.34
  229.6 1.8 collective-permute-done.36
  231.3 0.6 fusion.14
  (110 shorter events, 6.0 us)
Async XLA Ops:
  7.2 17.7 %copy-start = (bf16[768,512]{1,0:T(8,128)(2,1)S(1)}, bf16[768,512]{1,0:T(8,128)(2,1)}, u32[]{:S(2)}) copy-start(bf16[768,512]{1,0:T(8,128)(2,1)} %param.10) | copy-start | bytes 2359300
  7.2 56.9 %copy-start.1 = (bf16[896,512]{1,0:T(8,128)(2,1)S(1)}, bf16[896,512]{1,0:T(8,128)(2,1)}, u32[]{:S(2)}) copy-start(bf16[896,512]{1,0:T(8,128)(2,1)} %param.14) | copy-start | bytes 2752516
  7.2 17.7 %copy-start.9 = (bf16[512,64]{0,1:T(8,128)(2,1)S(1)}, bf16[512,64]{0,1:T(8,128)(2,1)}, u32[]{:S(2)}) copy-start(bf16[512,64]{0,1:T(8,128)(2,1)} %param.16) | copy-start | bytes 196612
  7.2 50.0 %all-gather.7.cloned.1.call-start = ((), (), s32[]{:S(2)}) async-start(), calls=%async_computation.2 | async-start | bytes 4587520 | tf_op jit(solution)/shard_map/all_gather | solution.py:263
  7.9 95.1 %all-gather.9.cloned.1.call-start = ((), (), s32[]{:S(2)}) async-start(), calls=%async_computation.3 | async-start | bytes 2293760 | tf_op jit(solution)/shard_map/all_gather | solution.py:263
  8.0 47.8 %collective-permute-start = (bf16[768,512]{1,0:T(8,128)(2,1)}, bf16[768,512]{1,0:T(8,128)(2,1)}, u32[]{:S(2)}, u32[]{:S(2)}) collective-permute-start(bf16[768,512]{1,0:T(8,128)(2,1)} %refs_1_.1), channel_id=1, source_target_pairs={{0,4},{16,28},{1,5},{17,29},{2,6},{18,30},{3,7},{19,31},{32,36},{4... | collective-permute-start | bytes 2359304 | tf_op jit(solution)/shard_map/ppermute | solution.py:27
  10.0 45.8 %collective-permute-start.1 = (bf16[768,512]{1,0:T(8,128)(2,1)}, bf16[768,512]{1,0:T(8,128)(2,1)}, u32[]{:S(2)}, u32[]{:S(2)}) collective-permute-start(bf16[768,512]{1,0:T(8,128)(2,1)} %refs_1_.1), channel_id=1, source_target_pairs={{0,1},{16,19},{1,2},{17,16},{2,3},{18,17},{3,0},{19,18},{32,33},{4... | collective-permute-start | bytes 2359304 | tf_op jit(solution)/shard_map/ppermute | solution.py:27
  11.5 44.3 %collective-permute-start.2 = (bf16[768,512]{1,0:T(8,128)(2,1)}, bf16[768,512]{1,0:T(8,128)(2,1)}, u32[]{:S(2)}, u32[]{:S(2)}) collective-permute-start(bf16[768,512]{1,0:T(8,128)(2,1)} %refs_1_.1), channel_id=1, source_target_pairs={{0,3},{16,17},{1,0},{17,18},{2,1},{18,19},{3,2},{19,16},{32,35},{4... | collective-permute-start | bytes 2359304 | tf_op jit(solution)/shard_map/ppermute | solution.py:27
  13.2 42.6 %collective-permute-start.3 = (bf16[768,512]{1,0:T(8,128)(2,1)}, bf16[768,512]{1,0:T(8,128)(2,1)}, u32[]{:S(2)}, u32[]{:S(2)}) collective-permute-start(bf16[768,512]{1,0:T(8,128)(2,1)} %refs_1_.1), channel_id=1, source_target_pairs={{0,2},{16,18},{1,3},{17,19},{2,0},{18,16},{3,1},{19,17},{32,34},{4... | collective-permute-start | bytes 2359304 | tf_op jit(solution)/shard_map/ppermute | solution.py:27
  16.9 38.9 %collective-permute-start.4 = (bf16[448,512]{1,0:T(8,128)(2,1)}, bf16[448,512]{1,0:T(8,128)(2,1)}, u32[]{:S(2)}, u32[]{:S(2)}) collective-permute-start(bf16[448,512]{1,0:T(8,128)(2,1)} %slice.28), channel_id=1, source_target_pairs={{0,128},{16,144},{1,129},{17,145},{2,130},{18,146},{3,131},{19,147... | collective-permute-start | bytes 1376264 | tf_op jit(solution)/shard_map/ppermute | solution.py:27
  25.6 85.1 %copy-start.3 = (bf16[768,896]{1,0:T(8,128)(2,1)S(1)}, bf16[768,896]{1,0:T(8,128)(2,1)}, u32[]{:S(2)}) copy-start(bf16[768,896]{1,0:T(8,128)(2,1)} %param.12) | copy-start | bytes 4128772
  25.6 85.1 %copy-start.10 = (bf16[896,64]{0,1:T(8,128)(2,1)S(1)}, bf16[896,64]{0,1:T(8,128)(2,1)}, u32[]{:S(2)}) copy-start(bf16[896,64]{0,1:T(8,128)(2,1)} %param.15) | copy-start | bytes 344068
  57.2 79.0 %all-gather.11.cloned.1.call-start = ((), (), s32[]{:S(2)}) async-start(), calls=%async_computation.4 | async-start | bytes 2293760 | tf_op jit(solution)/shard_map/all_gather | solution.py:263
  57.2 45.8 %collective-permute-start.5 = (bf16[768,512]{1,0:T(8,128)(2,1)}, bf16[768,512]{1,0:T(8,128)(2,1)}, u32[]{:S(2)}, u32[]{:S(2)}) collective-permute-start(bf16[768,512]{1,0:T(8,128)(2,1)} %collective-permute-done.refs_5_), channel_id=1, source_target_pairs={{0,4},{16,28},{1,5},{17,29},{2,6},{18,30},{3,7},{19,31},{32,36},{4... | collective-permute-start | bytes 2359304 | tf_op jit(solution)/shard_map/ppermute | solution.py:27
  59.0 44.0 %collective-permute-start.6 = (bf16[768,512]{1,0:T(8,128)(2,1)}, bf16[768,512]{1,0:T(8,128)(2,1)}, u32[]{:S(2)}, u32[]{:S(2)}) collective-permute-start(bf16[768,512]{1,0:T(8,128)(2,1)} %collective-permute-done.refs_5_), channel_id=1, source_target_pairs={{0,1},{16,19},{1,2},{17,16},{2,3},{18,17},{3,0},{19,18},{32,33},{4... | collective-permute-start | bytes 2359304 | tf_op jit(solution)/shard_map/ppermute | solution.py:27
  60.5 42.5 %collective-permute-start.7 = (bf16[768,512]{1,0:T(8,128)(2,1)}, bf16[768,512]{1,0:T(8,128)(2,1)}, u32[]{:S(2)}, u32[]{:S(2)}) collective-permute-start(bf16[768,512]{1,0:T(8,128)(2,1)} %collective-permute-done.refs_5_), channel_id=1, source_target_pairs={{0,3},{16,17},{1,0},{17,18},{2,1},{18,19},{3,2},{19,16},{32,35},{4... | collective-permute-start | bytes 2359304 | tf_op jit(solution)/shard_map/ppermute | solution.py:27
  62.3 40.8 %collective-permute-start.8 = (bf16[768,512]{1,0:T(8,128)(2,1)}, bf16[768,512]{1,0:T(8,128)(2,1)}, u32[]{:S(2)}, u32[]{:S(2)}) collective-permute-start(bf16[768,512]{1,0:T(8,128)(2,1)} %collective-permute-done.refs_5_), channel_id=1, source_target_pairs={{0,2},{16,18},{1,3},{17,19},{2,0},{18,16},{3,1},{19,17},{32,34},{4... | collective-permute-start | bytes 2359304 | tf_op jit(solution)/shard_map/ppermute | solution.py:27
  64.9 38.2 %collective-permute-start.9 = (bf16[448,512]{1,0:T(8,128)(2,1)}, bf16[448,512]{1,0:T(8,128)(2,1)S(1)}, u32[]{:S(2)}, u32[]{:S(2)}) collective-permute-start(bf16[448,512]{1,0:T(8,128)(2,1)} %slice.29), channel_id=1, source_target_pairs={{0,128},{16,144},{1,129},{17,145},{2,130},{18,146},{3,131},{19,147... | collective-permute-start | bytes 1376264 | tf_op jit(solution)/shard_map/ppermute | solution.py:27
  103.0 0.8 copy-start.7
  103.1 33.1 %collective-permute-start.14 = (bf16[4,896,512]{2,1,0:T(8,128)(2,1)}, bf16[4,896,512]{2,1,0:T(8,128)(2,1)}, u32[]{:S(2)}, u32[]{:S(2)}) collective-permute-start(bf16[4,896,512]{2,1,0:T(8,128)(2,1)} %bitcast.94), channel_id=1, source_target_pairs={{0,16},{16,0},{1,17},{17,1},{2,18},{18,2},{3,19},{19,3},{32,48},{4... | collective-permute-start | bytes 11010056 | tf_op jit(solution)/shard_map/ppermute | solution.py:27
  103.9 32.2 %collective-permute-start.10 = (bf16[768,512]{1,0:T(8,128)(2,1)}, bf16[768,512]{1,0:T(8,128)(2,1)}, u32[]{:S(2)}, u32[]{:S(2)}) collective-permute-start(bf16[768,512]{1,0:T(8,128)(2,1)} %collective-permute-done.5.refs_9_), channel_id=1, source_target_pairs={{0,4},{16,28},{1,5},{17,29},{2,6},{18,30},{3,7},{19,31},{32,36},{4... | collective-permute-start | bytes 2359304 | tf_op jit(solution)/shard_map/ppermute | solution.py:27
  104.0 32.1 %collective-permute-start.11 = (bf16[768,512]{1,0:T(8,128)(2,1)}, bf16[768,512]{1,0:T(8,128)(2,1)}, u32[]{:S(2)}, u32[]{:S(2)}) collective-permute-start(bf16[768,512]{1,0:T(8,128)(2,1)} %collective-permute-done.5.refs_9_), channel_id=1, source_target_pairs={{0,1},{16,19},{1,2},{17,16},{2,3},{18,17},{3,0},{19,18},{32,33},{4... | collective-permute-start | bytes 2359304 | tf_op jit(solution)/shard_map/ppermute | solution.py:27
  105.7 30.4 %collective-permute-start.12 = (bf16[768,512]{1,0:T(8,128)(2,1)}, bf16[768,512]{1,0:T(8,128)(2,1)}, u32[]{:S(2)}, u32[]{:S(2)}) collective-permute-start(bf16[768,512]{1,0:T(8,128)(2,1)} %collective-permute-done.5.refs_9_), channel_id=1, source_target_pairs={{0,3},{16,17},{1,0},{17,18},{2,1},{18,19},{3,2},{19,16},{32,35},{4... | collective-permute-start | bytes 2359304 | tf_op jit(solution)/shard_map/ppermute | solution.py:27
  108.6 4.5 %copy-start.4 = (bf16[768,896]{1,0:T(8,128)(2,1)S(1)}, bf16[768,896]{1,0:T(8,128)(2,1)}, u32[]{:S(2)}) copy-start(bf16[768,896]{1,0:T(8,128)(2,1)} %param.12) | copy-start | bytes 4128772
  108.6 4.5 %copy-start.5 = (bf16[768,896]{1,0:T(8,128)(2,1)S(1)}, bf16[768,896]{1,0:T(8,128)(2,1)}, u32[]{:S(2)}) copy-start(bf16[768,896]{1,0:T(8,128)(2,1)} %param.11) | copy-start | bytes 4128772
  108.6 26.6 %collective-permute-start.13 = (bf16[768,512]{1,0:T(8,128)(2,1)S(1)}, bf16[768,512]{1,0:T(8,128)(2,1)S(1)}, u32[]{:S(2)}, u32[]{:S(2)}) collective-permute-start(bf16[768,512]{1,0:T(8,128)(2,1)S(1)} %broadcast_select_fusion), channel_id=1, source_target_pairs={{0,2},{16,28},{1,3},{17,29},{2,0},{18,30},{3,1},{19,31},{32,34},{4... | collective-permute-start | bytes 2359304 | tf_op jit(solution)/shard_map/ppermute | solution.py:27
  113.0 23.2 %copy-start.2 = (bf16[1792,512]{1,0:T(8,128)(2,1)S(1)}, bf16[1792,512]{1,0:T(8,128)(2,1)}, u32[]{:S(2)}) copy-start(bf16[1792,512]{1,0:T(8,128)(2,1)} %all-gather.9.cloned.1.call-done) | copy-start | bytes 5505028
  113.1 23.9 %copy-start.12 = (s32[6,2]{0,1:T(2,128)S(1)}, s32[6,2]{0,1:T(2,128)}, u32[]{:S(2)}) copy-start(s32[6,2]{0,1:T(2,128)} %param.18) | copy-start | bytes 148
  113.1 24.0 %copy-start.13 = (s32[6]{0:T(128)S(1)}, s32[6]{0:T(128)}, u32[]{:S(2)}) copy-start(s32[6]{0:T(128)} %param.19) | copy-start | bytes 76
  135.2 0.9 copy-start.15
  136.2 8.7 %collective-permute-start.18 = (bf16[4,448,512]{2,1,0:T(8,128)(2,1)S(1)}, bf16[4,448,512]{2,1,0:T(8,128)(2,1)}, u32[]{:S(2)}, u32[]{:S(2)}) collective-permute-start(bf16[4,448,512]{2,1,0:T(8,128)(2,1)S(1)} %bitcast.99), channel_id=1, source_target_pairs={{0,16},{16,0},{1,17},{17,1},{2,18},{18,2},{3,19},{19,3},{32,48},{4... | collective-permute-start | bytes 5505032 | tf_op jit(solution)/shard_map/ppermute | solution.py:27
  136.3 8.6 %collective-permute-start.19 = (bf16[4,448,512]{2,1,0:T(8,128)(2,1)}, bf16[4,448,512]{2,1,0:T(8,128)(2,1)}, u32[]{:S(2)}, u32[]{:S(2)}) collective-permute-start(bf16[4,448,512]{2,1,0:T(8,128)(2,1)} %bitcast.100), channel_id=1, source_target_pairs={{0,16},{16,0},{1,17},{17,1},{2,18},{18,2},{3,19},{19,3},{32,48},{4... | collective-permute-start | bytes 5505032 | tf_op jit(solution)/shard_map/ppermute | solution.py:27
  137.4 7.5 %copy-start.14 = (s32[16]{0:T(128)}, s32[16]{0:T(128)S(1)}, u32[]{:S(2)}) copy-start(s32[16]{0:T(128)S(1)} %fusion.16) | copy-start | bytes 196
  138.9 22.8 %collective-permute-start.15 = (bf16[768,512]{1,0:T(8,128)(2,1)}, bf16[768,512]{1,0:T(8,128)(2,1)}, u32[]{:S(2)}, u32[]{:S(2)}) collective-permute-start(bf16[768,512]{1,0:T(8,128)(2,1)} %collective-permute-done.10.refs_1_), channel_id=1, source_target_pairs={{0,1},{16,19},{1,2},{17,16},{2,3},{18,17},{3,0},{19,18},{32,33},{4... | collective-permute-start | bytes 2359304 | tf_op jit(solution)/shard_map/ppermute | solution.py:27
  139.7 22.1 %collective-permute-start.16 = (bf16[768,512]{1,0:T(8,128)(2,1)}, bf16[768,512]{1,0:T(8,128)(2,1)}, u32[]{:S(2)}, u32[]{:S(2)}) collective-permute-start(bf16[768,512]{1,0:T(8,128)(2,1)} %collective-permute-done.10.refs_1_), channel_id=1, source_target_pairs={{0,3},{16,17},{1,0},{17,18},{2,1},{18,19},{3,2},{19,16},{32,35},{4... | collective-permute-start | bytes 2359304 | tf_op jit(solution)/shard_map/ppermute | solution.py:27
  142.3 19.5 %collective-permute-start.17 = (bf16[768,512]{1,0:T(8,128)(2,1)}, bf16[768,512]{1,0:T(8,128)(2,1)S(1)}, u32[]{:S(2)}, u32[]{:S(2)}) collective-permute-start(bf16[768,512]{1,0:T(8,128)(2,1)} %copy-done.15), channel_id=1, source_target_pairs={{0,4},{16,28},{1,5},{17,29},{2,6},{18,30},{3,7},{19,31},{32,36},{4... | collective-permute-start | bytes 2359304 | tf_op jit(solution)/shard_map/ppermute | solution.py:27
  161.9 0.9 copy-start.6
  181.7 33.5 %copy-start.8 = (bf16[256,512]{1,0:T(8,128)(2,1)S(1)}, bf16[256,512]{1,0:T(8,128)(2,1)}, u32[]{:S(2)}) copy-start(bf16[256,512]{1,0:T(8,128)(2,1)} %param.17) | copy-start | bytes 786436
  181.8 6.6 %collective-permute-start.20 = (f32[2,6,8,128]{3,2,1,0:T(8,128)}, f32[2,6,8,128]{3,2,1,0:T(8,128)S(1)}, u32[]{:S(2)}, u32[]{:S(2)}) collective-permute-start(f32[2,6,8,128]{3,2,1,0:T(8,128)} %get-tuple-element.59), channel_id=1, source_target_pairs={{0,1},{16,17},{1,2},{17,18},{2,3},{18,19},{3,0},{19,16},{32,33},{4... | collective-permute-start | bytes 147464 | tf_op jit(solution)/shard_map/ppermute | solution.py:27
  182.1 6.3 %collective-permute-start.21 = (f32[2,6,8,128]{3,2,1,0:T(8,128)}, f32[2,6,8,128]{3,2,1,0:T(8,128)S(1)}, u32[]{:S(2)}, u32[]{:S(2)}) collective-permute-start(f32[2,6,8,128]{3,2,1,0:T(8,128)} %get-tuple-element.60), channel_id=1, source_target_pairs={{0,2},{16,18},{1,3},{17,19},{2,0},{18,16},{3,1},{19,17},{32,34},{4... | collective-permute-start | bytes 147464 | tf_op jit(solution)/shard_map/ppermute | solution.py:27
  184.9 4.3 %collective-permute-start.22 = (f32[2,6,8,128]{3,2,1,0:T(8,128)}, f32[2,6,8,128]{3,2,1,0:T(8,128)S(1)}, u32[]{:S(2)}, u32[]{:S(2)}) collective-permute-start(f32[2,6,8,128]{3,2,1,0:T(8,128)} %get-tuple-element.61), channel_id=1, source_target_pairs={{0,3},{16,19},{1,0},{17,16},{2,1},{18,17},{3,2},{19,18},{32,35},{4... | collective-permute-start | bytes 147464 | tf_op jit(solution)/shard_map/ppermute | solution.py:27
  190.0 5.8 %collective-permute-start.23 = (f32[6,8,128]{2,1,0:T(8,128)S(1)}, f32[6,8,128]{2,1,0:T(8,128)S(1)}, u32[]{:S(2)}, u32[]{:S(2)}) collective-permute-start(f32[6,8,128]{2,1,0:T(8,128)S(1)} %get-tuple-element.65), channel_id=1, source_target_pairs={{0,4},{16,20},{1,5},{17,21},{2,6},{18,22},{3,7},{19,23},{32,36},{4... | collective-permute-start | bytes 73736 | tf_op jit(solution)/shard_map/ppermute | solution.py:27
  191.7 5.0 %collective-permute-start.24 = (f32[6,8,128]{2,1,0:T(8,128)S(1)}, f32[6,8,128]{2,1,0:T(8,128)S(1)}, u32[]{:S(2)}, u32[]{:S(2)}) collective-permute-start(f32[6,8,128]{2,1,0:T(8,128)S(1)} %get-tuple-element.67), channel_id=1, source_target_pairs={{0,8},{16,24},{1,9},{17,25},{2,10},{18,26},{3,11},{19,27},{32,40},... | collective-permute-start | bytes 73736 | tf_op jit(solution)/shard_map/ppermute | solution.py:27
  193.3 3.8 %collective-permute-start.25 = (f32[6,8,128]{2,1,0:T(8,128)S(1)}, f32[6,8,128]{2,1,0:T(8,128)S(1)}, u32[]{:S(2)}, u32[]{:S(2)}) collective-permute-start(f32[6,8,128]{2,1,0:T(8,128)S(1)} %get-tuple-element.66), channel_id=1, source_target_pairs={{0,12},{16,28},{1,13},{17,29},{2,14},{18,30},{3,15},{19,31},{32,44... | collective-permute-start | bytes 73736 | tf_op jit(solution)/shard_map/ppermute | solution.py:27
  197.4 34.6 %copy-start.11 = (f32[6,512]{1,0:T(8,128)}, f32[6,512]{1,0:T(8,128)S(1)}, u32[]{:S(2)}) copy-start(f32[6,512]{1,0:T(8,128)S(1)} %reshape.86) | copy-start | bytes 36868
  197.4 7.7 %collective-permute-start.26 = (f32[6,512]{1,0:T(8,128)S(1)}, f32[6,512]{1,0:T(8,128)S(1)}, u32[]{:S(2)}, u32[]{:S(2)}) collective-permute-start(f32[6,512]{1,0:T(8,128)S(1)} %reshape.86), channel_id=1, source_target_pairs={{0,128},{16,144},{1,129},{17,145},{2,130},{18,146},{3,131},{19,147... | collective-permute-start | bytes 36872 | tf_op jit(solution)/shard_map/ppermute | solution.py:27
  205.1 3.9 %collective-permute-start.27 = (f32[2,6,512]{2,1,0:T(8,128)S(1)}, f32[2,6,512]{2,1,0:T(8,128)S(1)}, u32[]{:S(2)}, u32[]{:S(2)}) collective-permute-start(f32[2,6,512]{2,1,0:T(8,128)S(1)} %bitcast_dynamic-update-slice_fusion.6), channel_id=1, source_target_pairs={{0,32},{16,48},{1,33},{17,49},{2,34},{18,50},{3,35},{19,51},{32,64... | collective-permute-start | bytes 73736 | tf_op jit(solution)/shard_map/ppermute | solution.py:27
  207.3 5.4 %collective-permute-start.28 = (f32[2,6,512]{2,1,0:T(8,128)S(1)}, f32[2,6,512]{2,1,0:T(8,128)S(1)}, u32[]{:S(2)}, u32[]{:S(2)}) collective-permute-start(f32[2,6,512]{2,1,0:T(8,128)S(1)} %bitcast_dynamic-update-slice_fusion.6), channel_id=1, source_target_pairs={{0,64},{16,80},{1,65},{17,81},{2,66},{18,82},{3,67},{19,83},{32,96... | collective-permute-start | bytes 73736 | tf_op jit(solution)/shard_map/ppermute | solution.py:27
  208.7 5.1 %collective-permute-start.29 = (f32[2,6,512]{2,1,0:T(8,128)S(1)}, f32[2,6,512]{2,1,0:T(8,128)S(1)}, u32[]{:S(2)}, u32[]{:S(2)}) collective-permute-start(f32[2,6,512]{2,1,0:T(8,128)S(1)} %bitcast_dynamic-update-slice_fusion.6), channel_id=1, source_target_pairs={{0,96},{16,112},{1,97},{17,113},{2,98},{18,114},{3,99},{19,115},{3... | collective-permute-start | bytes 73736 | tf_op jit(solution)/shard_map/ppermute | solution.py:27
  213.8 1.3 collective-permute-start.30
  215.8 5.1 %collective-permute-start.31 = (f32[4,6,256]{2,0,1:T(4,128)S(1)}, f32[4,6,256]{2,0,1:T(4,128)S(1)}, u32[]{:S(2)}, u32[]{:S(2)}) collective-permute-start(f32[4,6,256]{2,0,1:T(4,128)S(1)} %get-tuple-element.62), channel_id=1, source_target_pairs={{0,1},{16,17},{1,2},{17,18},{2,3},{18,19},{3,0},{19,16},{32,33},{4... | collective-permute-start | bytes 73736 | tf_op jit(solution)/shard_map/ppermute | solution.py:27
  217.4 5.3 %collective-permute-start.32 = (f32[4,6,256]{2,0,1:T(4,128)S(1)}, f32[4,6,256]{2,0,1:T(4,128)S(1)}, u32[]{:S(2)}, u32[]{:S(2)}) collective-permute-start(f32[4,6,256]{2,0,1:T(4,128)S(1)} %get-tuple-element.64), channel_id=1, source_target_pairs={{0,2},{16,18},{1,3},{17,19},{2,0},{18,16},{3,1},{19,17},{32,34},{4... | collective-permute-start | bytes 73736 | tf_op jit(solution)/shard_map/ppermute | solution.py:27
  219.7 3.8 %collective-permute-start.33 = (f32[4,6,256]{2,0,1:T(4,128)S(1)}, f32[4,6,256]{2,0,1:T(4,128)S(1)}, u32[]{:S(2)}, u32[]{:S(2)}) collective-permute-start(f32[4,6,256]{2,0,1:T(4,128)S(1)} %get-tuple-element.63), channel_id=1, source_target_pairs={{0,3},{16,19},{1,0},{17,16},{2,1},{18,17},{3,2},{19,18},{32,35},{4... | collective-permute-start | bytes 73736 | tf_op jit(solution)/shard_map/ppermute | solution.py:27
  223.6 5.5 %collective-permute-start.34 = (f32[6,256]{1,0:T(8,128)S(1)}, f32[6,256]{1,0:T(8,128)S(1)}, u32[]{:S(2)}, u32[]{:S(2)}) collective-permute-start(f32[6,256]{1,0:T(8,128)S(1)} %bitcast.109), channel_id=1, source_target_pairs={{0,4},{16,20},{1,5},{17,21},{2,6},{18,22},{3,7},{19,23},{32,36},{4... | collective-permute-start | bytes 18440 | tf_op jit(solution)/shard_map/ppermute | solution.py:27
  225.0 4.6 %collective-permute-start.35 = (f32[6,256]{1,0:T(8,128)S(1)}, f32[6,256]{1,0:T(8,128)S(1)}, u32[]{:S(2)}, u32[]{:S(2)}) collective-permute-start(f32[6,256]{1,0:T(8,128)S(1)} %bitcast.110), channel_id=1, source_target_pairs={{0,8},{16,24},{1,9},{17,25},{2,10},{18,26},{3,11},{19,27},{32,40},... | collective-permute-start | bytes 18440 | tf_op jit(solution)/shard_map/ppermute | solution.py:27
  227.7 3.7 %collective-permute-start.36 = (f32[6,256]{1,0:T(8,128)S(1)}, f32[6,256]{1,0:T(8,128)S(1)}, u32[]{:S(2)}, u32[]{:S(2)}) collective-permute-start(f32[6,256]{1,0:T(8,128)S(1)} %bitcast.111), channel_id=1, source_target_pairs={{0,12},{16,28},{1,13},{17,29},{2,14},{18,30},{3,15},{19,31},{32,44... | collective-permute-start | bytes 18440 | tf_op jit(solution)/shard_map/ppermute | solution.py:27
Sparse Core Ops, SparseCore 0:
  9.8 47.2 all-gather.6
  59.0 31.7 all-gather.8
  104.0 29.2 all-gather.10
